TPU v7x, 512 devices: a whole 4x8x8 slice. The times are simulated.
512 devices in a mesh: row: 32 (over z, x), col: 16 (over y, core).
Axes of the slice: x: 4, y: 8, z: 8, core: 2. Of those that a mesh axis runs over, the one named last changes fastest.
Arguments:
- pair: bfloat16 [512, 512, 128], P('row', 'col'), may hold values from -6 to 6
- gain_in: float32 [128], replicated, may hold values from 0.5 to 2
- w_in: bfloat16 [128, 512], replicated, may hold values from -0.5 to 0.5
- w_gate: bfloat16 [128, 128], replicated, may hold values from -0.5 to 0.5
- w_out: bfloat16 [128, 128], replicated, may hold values from -0.5 to 0.5
- gain_mid: float32 [128], replicated, may hold values from 0.5 to 2
- chain_len: int32 [4], replicated, may hold values from 1 to 16, 32 in all
- allowed: int32 [4, 4], replicated, may hold values 0 or 1
Outputs:
- update: bfloat16 [512, 512, 128], P('row', 'col')
Inputs may be any that keep to these rules, and one draw needn't show every extreme that they name: `chain_len`: chain lengths in blocks of 16 residues; they sum to 32 and the longest is 16.
All inputs are finite; a program needn't handle non-finite values.
Results may differ from a plain program's by a relative error of at most 0.019.
Values may be sent and summed in bfloat16 or wider, within the bound.
A program may use at most 64 MiB of HBM per device.

v0:
```python
import jax
import jax.numpy as jnp
from jax import lax
from jax.sharding import PartitionSpec as P

BLK = 16


def broadcast(array, axis, root):
    mine = lax.axis_index(axis) == root
    return lax.psum(jnp.where(mine, array, jnp.zeros_like(array)), axis)


def layer_norm(values, gain):
    mean = jnp.mean(values, axis=-1, keepdims=True)
    centered = values - mean
    var = jnp.mean(centered * centered, axis=-1, keepdims=True)
    return centered / jnp.sqrt(var + 1e-05) * gain


def chain_onehot(positions, chain_len):
    ends = jnp.cumsum(chain_len) * BLK
    chains = jnp.sum((positions[:, None] >= ends[None, :-1]).astype(jnp.int32), axis=1)
    labels = jnp.arange(chain_len.shape[0], dtype=jnp.int32)
    return (chains[:, None] == labels[None, :]).astype(jnp.float32)


def on_device(pair, gain_in, w_in, w_gate, w_out, gain_mid, chain_len, allowed):
    rows, cols, width = pair.shape
    hidden = w_out.shape[0]
    row_first = lax.axis_index("row") * rows
    col_first = lax.axis_index("col") * cols
    allowed_f = allowed.astype(jnp.float32)
    row_hot = chain_onehot(row_first + jnp.arange(rows, dtype=jnp.int32), chain_len)
    col_hot = chain_onehot(col_first + jnp.arange(cols, dtype=jnp.int32), chain_len)
    tile_mask = jnp.dot(jnp.dot(row_hot, allowed_f), col_hot.T)
    normed = layer_norm(pair.astype(jnp.float32), gain_in).astype(jnp.bfloat16)
    flat = normed.reshape(rows * cols, width)
    proj = jnp.dot(flat, w_in, preferred_element_type=jnp.float32).reshape(rows, cols, 4 * hidden)
    a_tile = (
        jax.nn.sigmoid(proj[..., :hidden]) * proj[..., hidden : 2 * hidden] * tile_mask[..., None]
    ).astype(jnp.bfloat16)
    b_tile = (
        jax.nn.sigmoid(proj[..., 2 * hidden : 3 * hidden])
        * proj[..., 3 * hidden :]
        * tile_mask[..., None]
    ).astype(jnp.bfloat16)
    b_rows = lax.all_gather(b_tile, "col", axis=1, tiled=True)
    ratio = lax.axis_size("row") // lax.axis_size("col")
    owners = [
        broadcast(b_rows, "row", lax.axis_index("col") * ratio + step) for step in range(ratio)
    ]
    b_panel = jnp.concatenate(owners, axis=0)
    mixed = jnp.einsum(
        "ikc,jkc->ijc",
        lax.all_gather(a_tile, "col", axis=1, tiled=True),
        b_panel,
        preferred_element_type=jnp.float32,
    )
    mixed_norm = layer_norm(mixed, gain_mid).astype(jnp.bfloat16).reshape(rows * cols, hidden)
    gate = jax.nn.sigmoid(jnp.dot(flat, w_gate, preferred_element_type=jnp.float32))
    result = gate * jnp.dot(mixed_norm, w_out, preferred_element_type=jnp.float32)
    return result.astype(jnp.bfloat16).reshape(rows, cols, width)


def solution(mesh):
    return jax.shard_map(
        on_device,
        mesh=mesh,
        in_specs=(P("row", "col", None), P(), P(), P(), P(), P(), P(), P()),
        out_specs=P("row", "col", None),
        check_vma=False,
    )
```

profile of v0, /device:TPU:1, one launch (start us, length us, event | category | flops | bytes accessed | tf_op | source)
XLA Modules:
  0.0 304.0 jit_solution(9197869155783661306)
XLA Ops:
  6.5 0.9 reduce-window.9
  7.4 0.1 convert_reduce_fusion.2
  7.5 0.1 convert_reduce_fusion.1
  7.6 1.0 convert_reduce_fusion
  8.7 1.2 fusion.9
  9.8 1.1 fusion.11
  11.0 0.3 fusion.22
  11.2 1.1 fusion.4
  12.3 0.9 fusion.13
  13.2 0.7 all-gather.5.cloned.1.call-update
  14.0 47.2 %all-gather.3.cloned.1.call-done = bf16[16,512,128]{2,1,0:T(8,128)(2,1)} async-done(((bf16[16,32,128]{2,1,0:T(8,128)(2,1)}), bf16[16,512,128]{2,1,0:T(8,128)(2,1)}) %all-gather.3.cloned.1.call-update) | async-done | bytes 2097168 | tf_op jit(solution)/shard_map/all_gather | solution.py:48
  61.2 4.0 %broadcast_select_fusion.1 = (bf16[16,512,128]{2,1,0:T(8,128)(2,1)}, bf16[16,512,128]{2,1,0:T(8,128)(2,1)}) fusion(bf16[16,512,128]{2,1,0:T(8,128)(2,1)} %all-gather.3.cloned.1.call-done, pred[]{:T(512)S(6)} %eq.32, pred[]{:T(512)S(6)} %eq.39), kind=kLoop, calls=%fused_computation.2 | loop fusion | flops 2097152 | bytes 6291458 | tf_op jit(solution)/shard_map/jit(_where)/select_n | solution.py:11
  65.2 0.7 copy-done.3
  65.9 0.2 fusion.2
  66.1 38.1 %all-gather.5.cloned.1.call-done = bf16[16,512,128]{2,1,0:T(8,128)(2,1)} async-done(((bf16[16,32,128]{2,1,0:T(8,128)(2,1)}), bf16[16,512,128]{2,1,0:T(8,128)(2,1)}) %all-gather.5.cloned.1.call-update) | async-done | bytes 2097168 | tf_op jit(solution)/shard_map/all_gather | solution.py:56
  104.2 3.4 %copy.15 = bf16[16,512,128]{1,0,2:T(8,128)(2,1)S(1)} copy(bf16[16,512,128]{2,1,0:T(8,128)(2,1)} %all-gather.5.cloned.1.call-done) | data formatting | bytes 4194304 | tf_op jit(solution)/shard_map/all_gather | solution.py:56
  107.6 172.3 %all-reduce.3.cloned.1.call-done = (bf16[16,512,128]{2,1,0:T(8,128)(2,1)}, bf16[16,512,128]{2,1,0:T(8,128)(2,1)}) async-done(((bf16[16,512,128]{2,1,0:T(8,128)(2,1)}, bf16[16,512,128]{2,1,0:T(8,128)(2,1)}), (bf16[16,512,128]{2,1,0:T(8,128)(2,1)}, bf16[16,512,128]{2,1,0:T(8,128)(2,1)})) %all-reduce.3.cloned.1.call-update) | async-done | bytes 4194320 | tf_op jit(solution)/shard_map/psum | solution.py:11
  279.9 4.5 %pad_maximum_fusion = bf16[32,512,128]{2,1,0:T(8,128)(2,1)} fusion(bf16[16,512,128]{2,1,0:T(8,128)(2,1)} %get-tuple-element.5, bf16[16,512,128]{2,1,0:T(8,128)(2,1)} %get-tuple-element.6), kind=kLoop, calls=%fused_computation | loop fusion | flops 2097152 | bytes 8388608 | tf_op jit(solution)/shard_map/concatenate | solution.py:53
  284.4 7.9 %copy.14 = bf16[32,512,128]{1,0,2:T(8,128)(2,1)} copy(bf16[32,512,128]{2,1,0:T(8,128)(2,1)} %pad_maximum_fusion) | data formatting | bytes 8388608 | tf_op jit(solution)/shard_map/concatenate | solution.py:53
  292.4 3.4 %fusion.29 = (f32[16,32]{1,0:T(8,128)S(1)}, f32[16,32,128]{1,0,2:T(8,128)S(1)}) fusion(bf16[32,512,128]{1,0,2:T(8,128)(2,1)} %copy.14, bf16[16,512,128]{1,0,2:T(8,128)(2,1)S(1)} %copy.15), kind=kOutput, calls=%fused_computation.52 | convolution fusion | flops 67173888 | bytes 6555648 | tf_op jit(solution)/shard_map/ikc,jkc->ijc/dot_general | solution.py:54
  295.8 0.2 multiply_reduce_fusion
  296.0 0.2 multiply_convert_fusion
  296.2 0.4 copy.16
  296.7 0.8 fusion.3
  (20 shorter events, 0.2 us)
Async XLA Ops:
  6.5 4.4 %copy-start = (bf16[128,512]{1,0:T(8,128)(2,1)S(1)}, bf16[128,512]{1,0:T(8,128)(2,1)}, u32[]{:S(2)}) copy-start(bf16[128,512]{1,0:T(8,128)(2,1)} %param.10) | copy-start | bytes 393220
  6.5 54.7 %all-gather.3.cloned.1.call-start = ((), (), s32[]{:S(2)}) async-start(), calls=%async_computation | async-start | bytes 2228224 | tf_op jit(solution)/shard_map/all_gather | solution.py:48
  13.2 91.0 %all-gather.5.cloned.1.call-start = ((), (), s32[]{:S(2)}) async-start(), calls=%async_computation.1 | async-start | bytes 2228224 | tf_op jit(solution)/shard_map/all_gather | solution.py:56
  14.0 266.0 %all-reduce.3.cloned.1.call-start = ((), (), s32[]{:S(2)}) async-start(), calls=%async_computation.2 | async-start | bytes 8388608 | tf_op jit(solution)/shard_map/psum | solution.py:11
  65.2 0.8 copy-start.3
  292.4 3.6 %copy-start.2 = (f32[128]{0:T(128)S(1)}, f32[128]{0:T(128)}, u32[]{:S(2)}) copy-start(f32[128]{0:T(128)} %param.13) | copy-start | bytes 1540
  295.8 0.9 copy-start.1
Sparse Core Ops, SparseCore 0:
  13.3 47.8 all-gather.2
  63.3 40.8 all-gather.4
  107.9 171.9 all-reduce.2
where the time goes:
time: 306 us; the launch traced here: 304 us
  waiting for transfers between devices  258 us (84%)
  other arithmetic  14.1 us (5%)
  between operations  13.2 us (4%)
  local copies, waits for them, and re-layouts  12.6 us (4%)
  matrix products  5.78 us (2%)
    psum x1, waiting for transfers between devices, broadcast(): return lax.psum(jnp.where(mine, array, jnp.zeros_like(array)), axis)  172 us
    all_gather x1, waiting for transfers between devices, on_device(): b_rows = lax.all_gather(b_tile, 'col', axis=1, tiled=True)  47.2 us
    all_gather x1, waiting for transfers between devices, on_device(): lax.all_gather(a_tile, 'col', axis=1, tiled=True)  38.1 us
    concatenate x1, local copies, waits for them, and re-layouts, on_device(): b_panel = jnp.concatenate(owners, axis=0)  7.94 us
  transfers between devices with their start and end apart: 3, of which 3 were waited for; matrix products, arithmetic and copies ran while one was open for 3% of the time, Pallas kernels for 0%

commit v1 on v0

v1 whole, which is shorter than its diff:
```python
import jax
import jax.numpy as jnp
from jax import lax
from jax.experimental import pallas as pl
from jax.experimental.pallas import tpu as pltpu
from jax.sharding import PartitionSpec as P

MESH = pl.DeviceIdType.MESH
F32, BF16 = jnp.float32, jnp.bfloat16
NX, NY, NZ = 4, 8, 8
NG = NY * NZ
EPS = 1e-5


def nt(a, b):
    return lax.dot_general(a, b, (((1,), (1,)), ((), ())), preferred_element_type=F32)


def sigmoid(v):
    return 1.0 / (1.0 + jnp.exp(-v))


def wait_bytes(ref, sem):
    pltpu.make_async_copy(ref, ref, sem).wait()


def kernel(
    pair, gin, win, wgate, wout, gmid, chain_len, allowed, out,
    nb, gate, wt, stage, send, recv, left, right, back, home, final, rows, sems,
):
    row, col = lax.axis_index("row"), lax.axis_index("col")
    z, x = lax.div(row, NX), lax.rem(row, NX)
    y, core = lax.div(col, 2), lax.rem(col, 2)
    me = y * NZ + z

    def plane(n):
        ty = lax.rem(y + lax.div(n, NZ), NY)
        tz = lax.rem(z + lax.rem(n, NZ), NZ)
        return (tz * NX + x, ty * 2 + core), ty * NZ + tz

    beside = (row, col + 1 - 2 * core)
    along = [(z * NX + lax.rem(x + d, NX), col) for d in range(1, NX)]

    barrier = pltpu.get_barrier_semaphore()

    def greet(n, carry):
        pl.semaphore_signal(barrier, inc=1, device_id=plane(n)[0], device_id_type=MESH)
        return carry

    for there in [beside, *along]:
        pl.semaphore_signal(barrier, inc=1, device_id=there, device_id_type=MESH)
    lax.fori_loop(1, NG, greet, 0)

    values = pair[...].reshape(512, 128).astype(F32)
    mean = jnp.mean(values, axis=1, keepdims=True)
    centered = values - mean
    var = jnp.mean(centered * centered, axis=1, keepdims=True)
    normed = (centered * lax.rsqrt(var + EPS) * gin[...]).astype(BF16)
    for i in range(16):
        nb[i % 8, i // 8, core] = normed[i * 32 : (i + 1) * 32]
    for b in range(4):
        wt[b * 128 : (b + 1) * 128, :] = win[:, b * 128 : (b + 1) * 128].astype(F32).T.astype(BF16)

    pl.semaphore_wait(barrier, NG - 1 + NX)
    swap = pltpu.make_async_remote_copy(
        nb.at[:, :, core], nb.at[:, :, core], sems.at[0], sems.at[1], device_id=beside, device_id_type=MESH
    )
    swap.start()

    gate[...] = sigmoid(jnp.dot(normed, wgate[...], preferred_element_type=F32)).reshape(16, 32, 128)

    lane = lax.broadcasted_iota(jnp.int32, (8, 128), 1)
    low = lane < 64
    column = y * 64 + jnp.where(low, lane, lane - 64)
    chain_row, chain_col, end = jnp.int32(0), jnp.zeros((8, 128), jnp.int32), jnp.int32(0)
    for c in range(3):
        end = end + chain_len[c]
        chain_row = chain_row + jnp.where(row >= end, 1, 0)
        chain_col = chain_col + jnp.where(column >= end * 16, 1, 0)
    mask = jnp.zeros((8, 128), F32)
    for b in range(4):
        pick = jnp.int32(0)
        for a in range(4):
            pick = jnp.where(chain_row == a, allowed[a, b], pick)
        mask = jnp.where(chain_col == b, pick.astype(F32), mask)
    mask = mask[0:1]

    half = pl.multiple_of(core * 64, 64)
    weights = jnp.concatenate([wt[pl.ds(b * 128 + half, 64), :] for b in range(4)], axis=0)
    swap.wait()
    for t in range(8):
        proj = nt(weights, nb[t].reshape(128, 128))
        stage[pl.ds(t, 64, stride=16), :] = sigmoid(proj[:64]) * proj[64:128] * mask
        stage[pl.ds(8 + t, 64, stride=16), :] = sigmoid(proj[128:192]) * proj[192:] * mask
    send[...] = stage[...].reshape(64, 16, 128).astype(BF16)

    def give(n, carry):
        there, index = plane(n)
        pltpu.make_async_remote_copy(
            send.at[index], recv.at[me], sems.at[2], sems.at[3], device_id=there, device_id_type=MESH
        ).start()
        return carry

    lax.fori_loop(1, NG, give, 0)
    pltpu.make_async_copy(send.at[me], recv.at[me], sems.at[3]).start()
    wait_bytes(recv, sems.at[3])

    wide = lax.broadcasted_iota(jnp.int32, (16, 128), 1) < 64
    for zz in range(8):
        for q in range(4):
            one = recv[(2 * q) * NZ + zz].astype(F32)
            two = recv[(2 * q + 1) * NZ + zz].astype(F32)
            first = jnp.where(wide, one, pltpu.roll(two, 64, 1))
            second = jnp.where(wide, pltpu.roll(one, 64, 1), two)
            at = slice(q * 128, (q + 1) * 128)
            left[zz, :, at] = jnp.concatenate([first[:8], second[:8]], axis=0).astype(BF16)
            right[zz, x, :, at] = jnp.concatenate([first[8:], second[8:]], axis=0).astype(BF16)

    for there in along:
        pltpu.make_async_remote_copy(
            right.at[:, x], right.at[:, x], sems.at[4], sems.at[5], device_id=there, device_id_type=MESH
        ).start()
    wait_bytes(right.at[:, pl.ds(0, NX - 1)], sems.at[5])

    lhs = left[...].reshape(128, 512)
    for p in range(4):
        sums = nt(lhs, right[2 * p : 2 * p + 2].reshape(128, 512))
        for zz in range(8):
            one, two = sums[zz * 16 : zz * 16 + 8], sums[zz * 16 + 8 : zz * 16 + 16]
            back[2 * p * NZ + zz] = jnp.where(low, one, pltpu.roll(two, 64, 1)).astype(BF16)
            back[(2 * p + 1) * NZ + zz] = jnp.where(low, pltpu.roll(one, 64, 1), two).astype(BF16)

    def give_back(n, carry):
        there, index = plane(n)
        pltpu.make_async_remote_copy(
            back.at[index], home.at[core, me], sems.at[6], sems.at[7], device_id=there, device_id_type=MESH
        ).start()
        return carry

    lax.fori_loop(1, NG, give_back, 0)
    pltpu.make_async_copy(back.at[me], home.at[core, me], sems.at[7]).start()
    wait_bytes(home.at[core], sems.at[7])
    swap2 = pltpu.make_async_remote_copy(
        home.at[core], home.at[core], sems.at[8], sems.at[9], device_id=beside, device_id_type=MESH
    )
    swap2.start()
    gain = jnp.broadcast_to(gmid[...], (128, 128)).T
    swap2.wait()

    final[...] = home[...].reshape(1024, 128).astype(F32)
    for t in range(8):
        mixed = final[pl.ds(t, 128, stride=8), :]
        mean = jnp.mean(mixed, axis=0, keepdims=True)
        centered = mixed - mean
        var = jnp.mean(centered * centered, axis=0, keepdims=True)
        mixed_norm = (centered * lax.rsqrt(var + EPS) * gain).astype(BF16)
        rows[t] = lax.dot_general(
            mixed_norm, wout[...], (((0,), (0,)), ((), ())), preferred_element_type=F32
        )
        for h in range(2):
            own = pl.multiple_of(h * 64 + core * 32, 32)
            out[8 * h + t] = (gate[8 * h + t] * rows[t, pl.ds(own, 32), :]).astype(BF16)

    wait_bytes(send.at[pl.ds(0, NG - 1)], sems.at[2])
    wait_bytes(right.at[:, pl.ds(0, NX - 1)], sems.at[4])
    wait_bytes(back.at[pl.ds(0, NG - 1)], sems.at[6])


def on_device(pair, gain_in, w_in, w_gate, w_out, gain_mid, chain_len, allowed):
    vmem, smem = pl.BlockSpec(memory_space=pltpu.VMEM), pl.BlockSpec(memory_space=pltpu.SMEM)
    return pl.pallas_call(
        kernel,
        out_shape=jax.ShapeDtypeStruct(pair.shape, pair.dtype),
        in_specs=[vmem] * 6 + [smem] * 2,
        out_specs=vmem,
        scratch_shapes=[
            pltpu.VMEM((8, 2, 2, 32, 128), BF16),
            pltpu.VMEM((16, 32, 128), F32),
            pltpu.VMEM((512, 128), BF16),
            pltpu.VMEM((1024, 128), F32),
            pltpu.VMEM((NG, 16, 128), BF16),
            pltpu.VMEM((NG, 16, 128), BF16),
            pltpu.VMEM((8, 16, 512), BF16),
            pltpu.VMEM((8, NX, 16, 512), BF16),
            pltpu.VMEM((NG, 8, 128), BF16),
            pltpu.VMEM((2, NG, 8, 128), BF16),
            pltpu.VMEM((1024, 128), F32),
            pltpu.VMEM((8, 128, 128), F32),
            pltpu.SemaphoreType.DMA((10,)),
        ],
        compiler_params=pltpu.CompilerParams(
            collective_id=0, has_side_effects=True, vmem_limit_bytes=32 * 2**20
        ),
    )(pair, gain_in.reshape(1, 128), w_in, w_gate, w_out, gain_mid.reshape(1, 128), chain_len, allowed)


def solution(mesh):
    return jax.shard_map(
        on_device,
        mesh=mesh,
        in_specs=(P("row", "col", None), P(), P(), P(), P(), P(), P(), P()),
        out_specs=P("row", "col", None),
        check_vma=False,
    )
```

time: 306 us -> 54.1 us (0.18)
  waiting for transfers between devices: 258 us -> 0 us
  Pallas kernels: 0 us -> 49.1 us
  other arithmetic: 14.1 us -> 0 us
  between operations: 13.2 us -> 0.03 us
  local copies, waits for them, and re-layouts: 12.6 us -> 4.67 us
  matrix products: 5.78 us -> 0 us
    psum x1 -> x0, waiting for transfers between devices: 172 us -> none  [broadcast(): return lax.psum(jnp.where(mine, array, jnp.zeros_like(array)), axis)]
    all_gather x2 -> x0, waiting for transfers between devices: 85.2 us -> none  [the longest x1 47.2 us: on_device(): b_rows = lax.all_gather(b_tile, 'col', axis=1, tiled=True)]
    pallas_call x0 -> x1, Pallas kernels: none -> 49.1 us  [on_device(): pl.pallas_call(kernel, out_shape=jax.ShapeDtypeStruct(pair.shape, pair.dt...]
    concatenate x1 -> x0, local copies, waits for them, and re-layouts: 7.94 us -> none  [on_device(): b_panel = jnp.concatenate(owners, axis=0)]
    dot_general x5 -> x0, matrix products: 5.78 us -> none  [the longest x1 3.4 us: on_device(): jnp.einsum('ikc,jkc->ijc', lax.all_gather(a_tile, 'col', axis=1, tiled=Tr...]
    concatenate x1 -> x0, other arithmetic: 4.51 us -> none  [on_device(): b_panel = jnp.concatenate(owners, axis=0)]
    select_n x1 -> x0, other arithmetic: 3.97 us -> none  [broadcast(): return lax.psum(jnp.where(mine, array, jnp.zeros_like(array)), axis)]
    unnamed x8 -> x17, local copies, waits for them, and re-layouts: 0.74 us -> 4.67 us
  transfers between devices with their start and end apart: 3 -> 0, of which waited for: 3 -> 0; matrix products, arithmetic and copies ran while one was open for 3% -> 0% of each run, Pallas kernels for 0% -> 0%
where the time goes in v1:
time: 54.1 us; the launch traced here: 53.8 us
  Pallas kernels  49.1 us (91%)
  local copies, waits for them, and re-layouts  4.67 us (9%)
    pallas_call x1, Pallas kernels, on_device(): pl.pallas_call(kernel, out_shape=jax.ShapeDtypeStruct(pair.shape, pair.dt...  49.1 us
    unnamed x17, local copies, waits for them, and re-layouts  4.67 us

profile of v1, /device:TPU:1, one launch (start us, length us, event | category | flops | bytes accessed | tf_op | source)
XLA Modules:
  0.0 53.8 jit_solution(17662771797233990512)
XLA Ops:
  0.0 0.0 copy-start.4
  0.0 0.0 copy-start.5
  0.0 0.0 copy-start.6
  0.0 0.0 copy-start.7
  0.0 0.7 %copy-done.4 = s32[4,4]{1,0:T(4,128)S(1)} copy-done((s32[4,4]{1,0:T(4,128)S(1)}, s32[4,4]{1,0:T(4,128)}, u32[]{:S(2)}) %copy-start.4) | copy-done | bytes 88
  0.7 0.0 copy-done.5
  0.7 0.0 copy-done.6
  0.7 0.0 copy-done.7
  0.7 0.0 copy-start
  0.7 0.9 %copy-done = bf16[16,32,128]{2,1,0:T(8,128)(2,1)S(1)} copy-done((bf16[16,32,128]{2,1,0:T(8,128)(2,1)S(1)}, bf16[16,32,128]{2,1,0:T(8,128)(2,1)}, u32[]{:S(2)}) %copy-start) | copy-done | bytes 131096
  1.6 0.0 copy-start.1
  1.6 0.9 %copy-done.1 = bf16[128,512]{1,0:T(8,128)(2,1)S(1)} copy-done((bf16[128,512]{1,0:T(8,128)(2,1)S(1)}, bf16[128,512]{1,0:T(8,128)(2,1)}, u32[]{:S(2)}) %copy-start.1) | copy-done | bytes 131096
  2.5 0.0 copy-start.2
  2.5 0.8 %copy-done.2 = bf16[128,128]{1,0:T(8,128)(2,1)S(1)} copy-done((bf16[128,128]{1,0:T(8,128)(2,1)S(1)}, bf16[128,128]{1,0:T(8,128)(2,1)}, u32[]{:S(2)}) %copy-start.2) | copy-done | bytes 32792
  3.3 0.0 copy-start.3
  3.3 0.8 %copy-done.3 = bf16[128,128]{1,0:T(8,128)(2,1)S(1)} copy-done((bf16[128,128]{1,0:T(8,128)(2,1)S(1)}, bf16[128,128]{1,0:T(8,128)(2,1)}, u32[]{:S(2)}) %copy-start.3) | copy-done | bytes 32792
  4.0 49.1 %shard_map.82 = bf16[16,32,128]{2,1,0:T(8,128)(2,1)S(1)} custom-call(bf16[16,32,128]{2,1,0:T(8,128)(2,1)S(1)} %copy-done, f32[1,128]{1,0:T(1,128)S(1)} %bitcast.2, bf16[128,512]{1,0:T(8,128)(2,1)S(1)} %copy-done.1, bf16[128,128]{1,0:T(8,128)(2,1)S(1)} %copy-done.2, bf16[128,128]{1,0:T(8,128)(2,1)S(1)} %copy-done.3, f32[1,128]{1,0:T(1,128)S(1)} %bitcast.3, ...), custom_call_target="tpu_custom_call" | custom-call | tf_op jit(solution)/shard_map/pallas_call | solution.py:171
  53.1 0.7 %copy.10 = bf16[16,32,128]{2,1,0:T(8,128)(2,1)} copy(bf16[16,32,128]{2,1,0:T(8,128)(2,1)S(1)} %shard_map.82) | data formatting | bytes 262144
Async XLA Ops:
  0.0 0.7 %copy-start.4 = (s32[4,4]{1,0:T(4,128)S(1)}, s32[4,4]{1,0:T(4,128)}, u32[]{:S(2)}) copy-start(s32[4,4]{1,0:T(4,128)} %allowed.1) | copy-start | bytes 196
  0.0 0.7 %copy-start.5 = (f32[128]{0:T(128)S(1)}, f32[128]{0:T(128)}, u32[]{:S(2)}) copy-start(f32[128]{0:T(128)} %param.9) | copy-start | bytes 1540
  0.0 0.7 %copy-start.6 = (f32[128]{0:T(128)S(1)}, f32[128]{0:T(128)}, u32[]{:S(2)}) copy-start(f32[128]{0:T(128)} %param.13) | copy-start | bytes 1540
  0.0 0.7 %copy-start.7 = (s32[4]{0:T(128)S(1)}, s32[4]{0:T(128)}, u32[]{:S(2)}) copy-start(s32[4]{0:T(128)} %chain_len.1) | copy-start | bytes 52
  0.7 0.9 %copy-start = (bf16[16,32,128]{2,1,0:T(8,128)(2,1)S(1)}, bf16[16,32,128]{2,1,0:T(8,128)(2,1)}, u32[]{:S(2)}) copy-start(bf16[16,32,128]{2,1,0:T(8,128)(2,1)} %pair.1) | copy-start | bytes 393220
  1.6 0.9 %copy-start.1 = (bf16[128,512]{1,0:T(8,128)(2,1)S(1)}, bf16[128,512]{1,0:T(8,128)(2,1)}, u32[]{:S(2)}) copy-start(bf16[128,512]{1,0:T(8,128)(2,1)} %win.1) | copy-start | bytes 393220
  2.5 0.8 %copy-start.2 = (bf16[128,128]{1,0:T(8,128)(2,1)S(1)}, bf16[128,128]{1,0:T(8,128)(2,1)}, u32[]{:S(2)}) copy-start(bf16[128,128]{1,0:T(8,128)(2,1)} %wgate.1) | copy-start | bytes 98308
  3.3 0.8 %copy-start.3 = (bf16[128,128]{1,0:T(8,128)(2,1)S(1)}, bf16[128,128]{1,0:T(8,128)(2,1)}, u32[]{:S(2)}) copy-start(bf16[128,128]{1,0:T(8,128)(2,1)} %wout.1) | copy-start | bytes 98308

commit v2 on v1

v2 whole, which is shorter than its diff:
```python
import jax
import jax.numpy as jnp
from jax import lax
from jax.experimental import pallas as pl
from jax.experimental.pallas import tpu as pltpu
from jax.sharding import PartitionSpec as P

MESH = pl.DeviceIdType.MESH
F32, BF16 = jnp.float32, jnp.bfloat16
NX, NY, NZ = 4, 8, 8
NG = NY * NZ
ORDER = (2, 1, 3, 0)
EPS = 1e-5
SWAP, LEFT, GATHER, BACK, SWAP2, SENT, LOAD = 0, 2, 3, 16, 17, 19, 24


def nt(a, b):
    return lax.dot_general(a, b, (((1,), (1,)), ((), ())), preferred_element_type=F32)


def sigmoid(v):
    return 1.0 / (1.0 + jnp.exp(-v))


def wait_bytes(ref, sem):
    pltpu.make_async_copy(ref, ref, sem).wait()


def kernel(
    pair_hbm, gin_hbm, win_hbm, wgate_hbm, wout_hbm, gmid_hbm, len_hbm, allowed_hbm, out,
    pair, gin, win, wgate, wout, gmid, chain_len, allowed,
    nb, gate, wt, stage, send_r, send_l, recv_r, recv_l, left, right, back, home, final, rows, sems, arrive,
):
    row, col = lax.axis_index("row"), lax.axis_index("col")
    z, x = lax.div(row, NX), lax.rem(row, NX)
    y, core = lax.div(col, 2), lax.rem(col, 2)
    zp, zb = lax.div(z, 2), lax.rem(z, 2)
    me = y * NZ + z

    def chip(ty, tz):
        return (tz * NX + x, ty * 2 + core)

    def plane(n):
        ty = lax.rem(y + lax.div(n, NZ), NY)
        tz = lax.rem(z + lax.rem(n, NZ), NZ)
        return chip(ty, tz), ty * NZ + tz

    def remote(src, dst, sent, arrived, there):
        return pltpu.make_async_remote_copy(src, dst, sent, arrived, device_id=there, device_id_type=MESH)

    beside = (row, col + 1 - 2 * core)
    x_up, x_down = lax.rem(x + 1, NX), lax.rem(x + NX - 1, NX)
    up, down = (z * NX + x_up, col), (z * NX + x_down, col)

    loads = [
        pltpu.make_async_copy(src, dst, sems.at[LOAD + n])
        for n, (src, dst) in enumerate(
            [(pair_hbm, pair), (gin_hbm, gin), (win_hbm, win), (wgate_hbm, wgate), (wout_hbm, wout),
             (gmid_hbm, gmid), (len_hbm, chain_len), (allowed_hbm, allowed)]
        )
    ]
    for load in loads:
        load.start()

    barrier = pltpu.get_barrier_semaphore()

    def greet(n, carry):
        pl.semaphore_signal(barrier, inc=1, device_id=plane(n)[0], device_id_type=MESH)
        return carry

    lax.fori_loop(1, NG, greet, 0)
    for there in (beside, up, down):
        pl.semaphore_signal(barrier, inc=1, device_id=there, device_id_type=MESH)

    loads[0].wait()
    loads[1].wait()
    values = pair[...].reshape(512, 128).astype(F32)
    mean = jnp.mean(values, axis=1, keepdims=True)
    centered = values - mean
    var = jnp.mean(centered * centered, axis=1, keepdims=True)
    normed = (centered * lax.rsqrt(var + EPS) * gin[...]).astype(BF16)
    for i in range(16):
        nb[i % 8, i // 8, core] = normed[i * 32 : (i + 1) * 32]
    loads[2].wait()
    for b in range(4):
        wt[b * 128 : (b + 1) * 128, :] = win[:, b * 128 : (b + 1) * 128].astype(F32).T.astype(BF16)
    for load in loads[3:]:
        load.wait()

    pl.semaphore_wait(barrier, NG + 2)
    swap = remote(nb.at[:, :, core], nb.at[:, :, core], sems.at[SWAP], sems.at[SWAP + 1], beside)
    swap.start()

    gate[...] = sigmoid(jnp.dot(normed, wgate[...], preferred_element_type=F32)).reshape(16, 32, 128)

    lane = lax.broadcasted_iota(jnp.int32, (8, 128), 1)
    low = lane < 64
    column = y * 64 + jnp.where(low, lane, lane - 64)
    chain_row, chain_col, end = jnp.int32(0), jnp.zeros((8, 128), jnp.int32), jnp.int32(0)
    for c in range(3):
        end = end + chain_len[c]
        chain_row = chain_row + jnp.where(row >= end, 1, 0)
        chain_col = chain_col + jnp.where(column >= end * 16, 1, 0)
    mask = jnp.zeros((8, 128), F32)
    for b in range(4):
        pick = jnp.int32(0)
        for a in range(4):
            pick = jnp.where(chain_row == a, allowed[a, b], pick)
        mask = jnp.where(chain_col == b, pick.astype(F32), mask)
    mask = mask[0:1]

    half = pl.multiple_of(core * 64, 64)

    def project(first, store):
        weights = jnp.concatenate(
            [wt[pl.ds(b * 128 + half, 64), :] for b in (first, first + 1)], axis=0
        )
        for t in range(8):
            proj = nt(weights, nb[t].reshape(128, 128))
            stage[pl.ds(t, 64, stride=8), :] = sigmoid(proj[:64]) * proj[64:] * mask
        store[...] = stage[...].reshape(64, 8, 128).astype(BF16)

    swap.wait()
    project(2, send_r)
    for r in ORDER:
        tp = lax.rem(zp + 4 - r, 4)
        for b in range(2):
            tz = tp * 2 + b

            def give(dy, carry, tz=tz, r=r):
                ty = lax.rem(y + dy, NY)
                remote(
                    send_r.at[ty * NZ + tz], recv_r.at[zp, zb, y], sems.at[SENT], arrive.at[r], chip(ty, tz)
                ).start()
                return carry

            lax.fori_loop(1, NY, give, 0)
            if r:
                give(0, 0)
            else:

                @pl.when(tz != z)
                def _(give=give):
                    give(0, 0)

    pltpu.make_async_copy(send_r.at[me], recv_r.at[zp, zb, y], arrive.at[0]).start()

    project(0, send_l)

    def give_left(n, carry):
        there, index = plane(n)
        remote(send_l.at[index], recv_l.at[z, y], sems.at[SENT + 1], sems.at[LEFT], there).start()
        return carry

    lax.fori_loop(1, NG, give_left, 0)
    pltpu.make_async_copy(send_l.at[me], recv_l.at[z, y], sems.at[LEFT]).start()

    def merge(one, two):
        one, two = one.astype(F32), two.astype(F32)
        first = jnp.where(low, one, pltpu.roll(two, 64, 1))
        second = jnp.where(low, pltpu.roll(one, 64, 1), two)
        return jnp.concatenate([first, second], axis=0).astype(BF16)

    def own(p):
        return right.at[p, :, x]

    for r in ORDER:
        p = lax.rem(zp + r, 4)
        wait_bytes(recv_r.at[p], arrive.at[r])
        for b in range(2):
            for q in range(4):
                right[p, b, x, :, q * 128 : (q + 1) * 128] = merge(recv_r[p, b, 2 * q], recv_r[p, b, 2 * q + 1])
        remote(own(p), own(p), sems.at[SENT + 2], sems.at[GATHER + r], up).start()
        remote(own(p), own(p), sems.at[SENT + 2], sems.at[GATHER + 4 + r], down).start()

    for n, r in enumerate(ORDER):
        p = lax.rem(zp + r, 4)
        came, there, source = ((GATHER, up, x_down), (GATHER + 4, down, x_up))[n % 2]
        wait_bytes(right.at[p, :, source], sems.at[came + r])
        remote(
            right.at[p, :, source], right.at[p, :, source], sems.at[SENT + 2], sems.at[GATHER + 8 + r], there
        ).start()

    wait_bytes(recv_l, sems.at[LEFT])
    for zz in range(8):
        for q in range(4):
            left[zz, :, q * 128 : (q + 1) * 128] = merge(recv_l[zz, 2 * q], recv_l[zz, 2 * q + 1])

    lhs = left[...].reshape(128, 512)
    x_far = lax.rem(x + 2, NX)
    for n, r in enumerate(ORDER):
        p = lax.rem(zp + r, 4)
        came, source = ((GATHER + 4, x_up), (GATHER, x_down))[n % 2]
        wait_bytes(right.at[p, :, source], sems.at[came + r])
        wait_bytes(right.at[p, :, x_far], sems.at[GATHER + 8 + r])
        sums = nt(lhs, right[p].reshape(128, 512))
        for zz in range(8):
            one, two = sums[zz * 16 : zz * 16 + 8], sums[zz * 16 + 8 : zz * 16 + 16]
            back[p, 0, zz] = jnp.where(low, one, pltpu.roll(two, 64, 1)).astype(BF16)
            back[p, 1, zz] = jnp.where(low, pltpu.roll(one, 64, 1), two).astype(BF16)
        for b in range(2):
            ty = p * 2 + b

            def give_back(dz, carry, ty=ty, p=p, b=b):
                tz = lax.rem(z + dz, NZ)
                remote(back.at[p, b, tz], home.at[core, me], sems.at[SENT + 3], sems.at[BACK], chip(ty, tz)).start()
                return carry

            lax.fori_loop(1, NZ, give_back, 0)

            @pl.when(ty != y)
            def _(give_back=give_back):
                give_back(0, 0)

    pltpu.make_async_copy(back.at[lax.div(y, 2), lax.rem(y, 2), z], home.at[core, me], sems.at[BACK]).start()
    gain = jnp.broadcast_to(gmid[...], (128, 128)).T
    wait_bytes(home.at[core], sems.at[BACK])
    swap2 = remote(home.at[core], home.at[core], sems.at[SWAP2], sems.at[SWAP2 + 1], beside)
    swap2.start()
    swap2.wait()

    final[...] = home[...].reshape(1024, 128).astype(F32)
    for t in range(8):
        mixed = final[pl.ds(t, 128, stride=8), :]
        mean = jnp.mean(mixed, axis=0, keepdims=True)
        centered = mixed - mean
        var = jnp.mean(centered * centered, axis=0, keepdims=True)
        mixed_norm = (centered * lax.rsqrt(var + EPS) * gain).astype(BF16)
        rows[t] = lax.dot_general(
            mixed_norm, wout[...], (((0,), (0,)), ((), ())), preferred_element_type=F32
        )
        for h in range(2):
            mine = pl.multiple_of(h * 64 + core * 32, 32)
            out[8 * h + t] = (gate[8 * h + t] * rows[t, pl.ds(mine, 32), :]).astype(BF16)

    wait_bytes(send_r.at[pl.ds(0, NG - 1)], sems.at[SENT])
    wait_bytes(send_l.at[pl.ds(0, NG - 1)], sems.at[SENT + 1])
    wait_bytes(right.at[:, :, pl.ds(0, 3)], sems.at[SENT + 2])
    wait_bytes(send_l.at[pl.ds(0, NG - 1)], sems.at[SENT + 3])


def on_device(pair, gain_in, w_in, w_gate, w_out, gain_mid, chain_len, allowed):
    operands = (pair, gain_in.reshape(1, 128), w_in, w_gate, w_out, gain_mid.reshape(1, 128))
    scalars = (chain_len, allowed)
    return pl.pallas_call(
        kernel,
        out_shape=jax.ShapeDtypeStruct(pair.shape, pair.dtype),
        in_specs=[pl.BlockSpec(memory_space=pl.ANY)] * 8,
        out_specs=pl.BlockSpec(memory_space=pltpu.VMEM),
        scratch_shapes=[
            *[pltpu.VMEM(a.shape, a.dtype) for a in operands],
            *[pltpu.SMEM(a.shape, a.dtype) for a in scalars],
            pltpu.VMEM((8, 2, 2, 32, 128), BF16),
            pltpu.VMEM((16, 32, 128), F32),
            pltpu.VMEM((512, 128), BF16),
            pltpu.VMEM((512, 128), F32),
            pltpu.VMEM((NG, 8, 128), BF16),
            pltpu.VMEM((NG, 8, 128), BF16),
            pltpu.VMEM((4, 2, NY, 8, 128), BF16),
            pltpu.VMEM((NZ, NY, 8, 128), BF16),
            pltpu.VMEM((NZ, 16, 512), BF16),
            pltpu.VMEM((4, 2, NX, 16, 512), BF16),
            pltpu.VMEM((4, 2, NZ, 8, 128), BF16),
            pltpu.VMEM((2, NG, 8, 128), BF16),
            pltpu.VMEM((1024, 128), F32),
            pltpu.VMEM((8, 128, 128), F32),
            pltpu.SemaphoreType.DMA((32,)),
            pltpu.SemaphoreType.DMA((4,)),
        ],
        compiler_params=pltpu.CompilerParams(
            collective_id=0, has_side_effects=True, vmem_limit_bytes=56 * 2**20
        ),
    )(*operands, *scalars)


def solution(mesh):
    return jax.shard_map(
        on_device,
        mesh=mesh,
        in_specs=(P("row", "col", None), P(), P(), P(), P(), P(), P(), P()),
        out_specs=P("row", "col", None),
        check_vma=False,
    )
```

time: 54.1 us -> 45.5 us (0.84)
  Pallas kernels: 49.1 us -> 43.8 us
  local copies, waits for them, and re-layouts: 4.67 us -> 1.57 us
    pallas_call x1, Pallas kernels: 49.1 us -> 43.8 us  [on_device(): pl.pallas_call(kernel, out_shape=jax.ShapeDtypeStruct(pair.shape, pair.dt...]
    unnamed x17 -> x1, local copies, waits for them, and re-layouts: 4.67 us -> 1.57 us
where the time goes in v2:
time: 45.5 us; the launch traced here: 45.4 us
  Pallas kernels  43.8 us (96%)
  local copies, waits for them, and re-layouts  1.57 us (3%)
    pallas_call x1, Pallas kernels, on_device(): pl.pallas_call(kernel, out_shape=jax.ShapeDtypeStruct(pair.shape, pair.dt...  43.8 us
    unnamed x1, local copies, waits for them, and re-layouts  1.57 us

profile of v2, /device:TPU:1, one launch (start us, length us, event | category | flops | bytes accessed | tf_op | source)
XLA Modules:
  0.0 45.4 jit_solution(14069918646682081820)
XLA Ops:
  0.0 43.8 %shard_map.82 = bf16[16,32,128]{2,1,0:T(8,128)(2,1)} custom-call(bf16[16,32,128]{2,1,0:T(8,128)(2,1)} %pair_hbm.1, f32[1,128]{1,0:T(1,128)} %bitcast.2, bf16[128,512]{1,0:T(8,128)(2,1)} %win_hbm.1, bf16[128,128]{1,0:T(8,128)(2,1)} %wgate_hbm.1, bf16[128,128]{1,0:T(8,128)(2,1)} %wout_hbm.1, f32[1,128]{1,0:T(1,128)} %bitcast.3, s32[4]{0:T(128)} %len_hbm.1, ...), custom_call_target="tpu_custom_call" | custom-call | tf_op jit(solution)/shard_map/pallas_call | solution.py:245
  43.8 1.6 %copy.10 = bf16[16,32,128]{2,1,0:T(8,128)(2,1)} copy(bf16[16,32,128]{2,1,0:T(8,128)(2,1)} %shard_map.82) | data formatting | bytes 262144

commit v3 on v2

--- a/solution.py
+++ b/solution.py
@@ -9,9 +9,9 @@
 F32, BF16 = jnp.float32, jnp.bfloat16
 NX, NY, NZ = 4, 8, 8
 NG = NY * NZ
-ORDER = (2, 1, 3, 0)
+ORDER = (0, 1, 3, 2)
 EPS = 1e-5
-SWAP, LEFT, GATHER, BACK, SWAP2, SENT, LOAD = 0, 2, 3, 16, 17, 19, 24
+SWAP, LEFT, GATHER, BACK, SWAP2, SENT, LOAD = 0, 2, 3, 15, 19, 21, 25
 
 
 def nt(a, b):
@@ -35,7 +35,7 @@
     z, x = lax.div(row, NX), lax.rem(row, NX)
     y, core = lax.div(col, 2), lax.rem(col, 2)
     zp, zb = lax.div(z, 2), lax.rem(z, 2)
-    me = y * NZ + z
+    me = z * NY + y
 
     def chip(ty, tz):
         return (tz * NX + x, ty * 2 + core)
@@ -43,14 +43,14 @@
     def plane(n):
         ty = lax.rem(y + lax.div(n, NZ), NY)
         tz = lax.rem(z + lax.rem(n, NZ), NZ)
-        return chip(ty, tz), ty * NZ + tz
+        return chip(ty, tz)
 
     def remote(src, dst, sent, arrived, there):
         return pltpu.make_async_remote_copy(src, dst, sent, arrived, device_id=there, device_id_type=MESH)
 
     beside = (row, col + 1 - 2 * core)
     x_up, x_down = lax.rem(x + 1, NX), lax.rem(x + NX - 1, NX)
-    up, down = (z * NX + x_up, col), (z * NX + x_down, col)
+    up, down, far = (z * NX + x_up, col), (z * NX + x_down, col), (z * NX + lax.rem(x + 2, NX), col)
 
     loads = [
         pltpu.make_async_copy(src, dst, sems.at[LOAD + n])
@@ -64,12 +64,9 @@
 
     barrier = pltpu.get_barrier_semaphore()
 
-    def greet(n, carry):
-        pl.semaphore_signal(barrier, inc=1, device_id=plane(n)[0], device_id_type=MESH)
-        return carry
-
-    lax.fori_loop(1, NG, greet, 0)
-    for there in (beside, up, down):
+    for n in range(1, NG):
+        pl.semaphore_signal(barrier, inc=1, device_id=plane(n), device_id_type=MESH)
+    for there in (beside, up, down, far):
         pl.semaphore_signal(barrier, inc=1, device_id=there, device_id_type=MESH)
 
     loads[0].wait()
@@ -87,7 +84,7 @@
     for load in loads[3:]:
         load.wait()
 
-    pl.semaphore_wait(barrier, NG + 2)
+    pl.semaphore_wait(barrier, NG + 3)
     swap = remote(nb.at[:, :, core], nb.at[:, :, core], sems.at[SWAP], sems.at[SWAP + 1], beside)
     swap.start()
 
@@ -122,37 +119,21 @@
 
     swap.wait()
     project(2, send_r)
-    for r in ORDER:
-        tp = lax.rem(zp + 4 - r, 4)
-        for b in range(2):
-            tz = tp * 2 + b
-
-            def give(dy, carry, tz=tz, r=r):
-                ty = lax.rem(y + dy, NY)
-                remote(
-                    send_r.at[ty * NZ + tz], recv_r.at[zp, zb, y], sems.at[SENT], arrive.at[r], chip(ty, tz)
-                ).start()
-                return carry
-
-            lax.fori_loop(1, NY, give, 0)
-            if r:
-                give(0, 0)
-            else:
-
-                @pl.when(tz != z)
-                def _(give=give):
-                    give(0, 0)
-
-    pltpu.make_async_copy(send_r.at[me], recv_r.at[zp, zb, y], arrive.at[0]).start()
+    others = [(dy, dz) for dz in reversed(range(NZ)) for dy in range(NY) if dy or dz]
+
+    for dy, dz in others:
+        ty, tz = lax.rem(y + dy, NY), lax.rem(z + dz, NZ)
+        remote(
+            send_r.at[tz * NY + ty], recv_r.at[zp, zb, y], sems.at[SENT], arrive.at[zp], chip(ty, tz)
+        ).start()
+    pltpu.make_async_copy(send_r.at[me], recv_r.at[zp, zb, y], arrive.at[zp]).start()
 
     project(0, send_l)
 
-    def give_left(n, carry):
-        there, index = plane(n)
-        remote(send_l.at[index], recv_l.at[z, y], sems.at[SENT + 1], sems.at[LEFT], there).start()
-        return carry
-
-    lax.fori_loop(1, NG, give_left, 0)
+    for dy, dz in others:
+        ty, tz = lax.rem(y + dy, NY), lax.rem(z + dz, NZ)
+        remote(send_l.at[tz * NY + ty], recv_l.at[z, y], sems.at[SENT + 1], sems.at[LEFT], chip(ty, tz)).start()
+
     pltpu.make_async_copy(send_l.at[me], recv_l.at[z, y], sems.at[LEFT]).start()
 
     def merge(one, two):
@@ -164,60 +145,61 @@
     def own(p):
         return right.at[p, :, x]
 
-    for r in ORDER:
-        p = lax.rem(zp + r, 4)
-        wait_bytes(recv_r.at[p], arrive.at[r])
+    x_far = lax.rem(x + 2, NX)
+    routes = [((GATHER, up, x_down), (GATHER + 4, x_up)), ((GATHER + 4, down, x_up), (GATHER, x_down))] * 2
+
+    def spread(p):
+        wait_bytes(recv_r.at[p], arrive.at[p])
         for b in range(2):
             for q in range(4):
                 right[p, b, x, :, q * 128 : (q + 1) * 128] = merge(recv_r[p, b, 2 * q], recv_r[p, b, 2 * q + 1])
-        remote(own(p), own(p), sems.at[SENT + 2], sems.at[GATHER + r], up).start()
-        remote(own(p), own(p), sems.at[SENT + 2], sems.at[GATHER + 4 + r], down).start()
-
-    for n, r in enumerate(ORDER):
-        p = lax.rem(zp + r, 4)
-        came, there, source = ((GATHER, up, x_down), (GATHER + 4, down, x_up))[n % 2]
-        wait_bytes(right.at[p, :, source], sems.at[came + r])
-        remote(
-            right.at[p, :, source], right.at[p, :, source], sems.at[SENT + 2], sems.at[GATHER + 8 + r], there
-        ).start()
-
+        remote(own(p), own(p), sems.at[SENT + 2], sems.at[GATHER + p], up).start()
+        remote(own(p), own(p), sems.at[SENT + 2], sems.at[GATHER + 4 + p], down).start()
+        remote(own(p), own(p), sems.at[SENT + 2], sems.at[GATHER + 8 + p], far).start()
+
+    def contract(p):
+        wait_bytes(right.at[p, :, x_down], sems.at[GATHER + p])
+        wait_bytes(right.at[p, :, x_up], sems.at[GATHER + 4 + p])
+        wait_bytes(right.at[p, :, x_far], sems.at[GATHER + 8 + p])
+        sums = nt(left[...].reshape(128, 512), right[p].reshape(128, 512))
+        for zz in range(8):
+            one, two = sums[zz * 16 : zz * 16 + 8], sums[zz * 16 + 8 : zz * 16 + 16]
+            back[p, 0, zz] = jnp.where(low, one, pltpu.roll(two, 64, 1)).astype(BF16)
+            back[p, 1, zz] = jnp.where(low, pltpu.roll(one, 64, 1), two).astype(BF16)
+        def give_back(b, tz):
+            remote(
+                back.at[p, b, tz], home.at[core, me], sems.at[SENT + 3], sems.at[BACK + zp], chip(p * 2 + b, tz)
+            ).start()
+
+        for dz in range(1, NZ):
+            for b in range(2):
+                give_back(b, lax.rem(z + dz, NZ))
+        for b in range(2):
+
+            @pl.when(p * 2 + b != y)
+            def _(b=b):
+                give_back(b, z)
+
+    c0, c1, c2, c3 = ORDER
+    spread(c0)
+    spread(c1)
+    spread(c2)
+    spread(c3)
     wait_bytes(recv_l, sems.at[LEFT])
     for zz in range(8):
         for q in range(4):
             left[zz, :, q * 128 : (q + 1) * 128] = merge(recv_l[zz, 2 * q], recv_l[zz, 2 * q + 1])
-
-    lhs = left[...].reshape(128, 512)
-    x_far = lax.rem(x + 2, NX)
-    for n, r in enumerate(ORDER):
-        p = lax.rem(zp + r, 4)
-        came, source = ((GATHER + 4, x_up), (GATHER, x_down))[n % 2]
-        wait_bytes(right.at[p, :, source], sems.at[came + r])
-        wait_bytes(right.at[p, :, x_far], sems.at[GATHER + 8 + r])
-        sums = nt(lhs, right[p].reshape(128, 512))
-        for zz in range(8):
-            one, two = sums[zz * 16 : zz * 16 + 8], sums[zz * 16 + 8 : zz * 16 + 16]
-            back[p, 0, zz] = jnp.where(low, one, pltpu.roll(two, 64, 1)).astype(BF16)
-            back[p, 1, zz] = jnp.where(low, pltpu.roll(one, 64, 1), two).astype(BF16)
-        for b in range(2):
-            ty = p * 2 + b
-
-            def give_back(dz, carry, ty=ty, p=p, b=b):
-                tz = lax.rem(z + dz, NZ)
-                remote(back.at[p, b, tz], home.at[core, me], sems.at[SENT + 3], sems.at[BACK], chip(ty, tz)).start()
-                return carry
-
-            lax.fori_loop(1, NZ, give_back, 0)
-
-            @pl.when(ty != y)
-            def _(give_back=give_back):
-                give_back(0, 0)
-
-    pltpu.make_async_copy(back.at[lax.div(y, 2), lax.rem(y, 2), z], home.at[core, me], sems.at[BACK]).start()
+    contract(c0)
+    contract(c1)
+    contract(c2)
+    contract(c3)
+    pltpu.make_async_copy(back.at[lax.div(y, 2), lax.rem(y, 2), z], home.at[core, me], sems.at[BACK + zp]).start()
     gain = jnp.broadcast_to(gmid[...], (128, 128)).T
-    wait_bytes(home.at[core], sems.at[BACK])
-    swap2 = remote(home.at[core], home.at[core], sems.at[SWAP2], sems.at[SWAP2 + 1], beside)
-    swap2.start()
-    swap2.wait()
+    for q in range(4):
+        part = home.at[core, pl.ds(q * 16, 16)]
+        wait_bytes(part, sems.at[BACK + q])
+        remote(part, part, sems.at[SWAP2], sems.at[SWAP2 + 1], beside).start()
+    wait_bytes(home.at[core], sems.at[SWAP2 + 1])
 
     final[...] = home[...].reshape(1024, 128).astype(F32)
     for t in range(8):
@@ -237,6 +219,7 @@
     wait_bytes(send_l.at[pl.ds(0, NG - 1)], sems.at[SENT + 1])
     wait_bytes(right.at[:, :, pl.ds(0, 3)], sems.at[SENT + 2])
     wait_bytes(send_l.at[pl.ds(0, NG - 1)], sems.at[SENT + 3])
+    wait_bytes(home.at[core], sems.at[SWAP2])
 
 
 def on_device(pair, gain_in, w_in, w_gate, w_out, gain_mid, chain_len, allowed):
@@ -264,13 +247,13 @@
             pltpu.VMEM((2, NG, 8, 128), BF16),
             pltpu.VMEM((1024, 128), F32),
             pltpu.VMEM((8, 128, 128), F32),
-            pltpu.SemaphoreType.DMA((32,)),
+            pltpu.SemaphoreType.DMA((33,)),
             pltpu.SemaphoreType.DMA((4,)),
         ],
         compiler_params=pltpu.CompilerParams(
-            collective_id=0, has_side_effects=True, vmem_limit_bytes=56 * 2**20
+            collective_id=0, has_side_effects=True, vmem_limit_bytes=32 * 2**20
         ),
-    )(*operands, *scalars)
+    )(*[pltpu.with_memory_space_constraint(a, pltpu.HBM) for a in (*operands, *scalars)])
 
 
 def solution(mesh):

time: 45.5 us -> 42.5 us (0.934)
  Pallas kernels: 43.8 us -> 41.7 us
  local copies, waits for them, and re-layouts: 1.57 us -> 0.66 us
    pallas_call x1, Pallas kernels: 43.8 us -> 41.7 us  [on_device(): pl.pallas_call(kernel, out_shape=jax.ShapeDtypeStruct(pair.shape, pair.dt...]
    unnamed x1, local copies, waits for them, and re-layouts: 1.57 us -> 0.66 us
where the time goes in v3:
time: 42.5 us; the launch traced here: 42.3 us
  Pallas kernels  41.7 us (98%)
  local copies, waits for them, and re-layouts  0.66 us (2%)
    pallas_call x1, Pallas kernels, on_device(): pl.pallas_call(kernel, out_shape=jax.ShapeDtypeStruct(pair.shape, pair.dt...  41.7 us

profile of v3, /device:TPU:1, one launch (start us, length us, event | category | flops | bytes accessed | tf_op | source)
XLA Modules:
  0.0 42.3 jit_solution(17920235709196000757)
XLA Ops:
  0.0 41.7 %shard_map.82 = bf16[16,32,128]{2,1,0:T(8,128)(2,1)S(1)} custom-call(bf16[16,32,128]{2,1,0:T(8,128)(2,1)} %pair_hbm.1, f32[1,128]{1,0:T(1,128)} %bitcast.2, bf16[128,512]{1,0:T(8,128)(2,1)} %win_hbm.1, bf16[128,128]{1,0:T(8,128)(2,1)} %wgate_hbm.1, bf16[128,128]{1,0:T(8,128)(2,1)} %wout_hbm.1, f32[1,128]{1,0:T(1,128)} %bitcast.3, s32[4]{0:T(128)} %len_hbm.1, ...), custom_call_target="tpu_custom_call" | custom-call | tf_op jit(solution)/shard_map/pallas_call | solution.py:228
  41.7 0.7 %copy.10 = bf16[16,32,128]{2,1,0:T(8,128)(2,1)} copy(bf16[16,32,128]{2,1,0:T(8,128)(2,1)S(1)} %shard_map.82) | data formatting | bytes 262144

commit v4 on v3

v4 whole, which is shorter than its diff:
```python
import jax
import jax.numpy as jnp
from jax import lax
from jax.experimental import pallas as pl
from jax.experimental.pallas import tpu as pltpu
from jax.sharding import PartitionSpec as P

MESH = pl.DeviceIdType.MESH
F32, BF16 = jnp.float32, jnp.bfloat16
NX, NY, NZ = 4, 8, 8
NG = NY * NZ
ORDER = (0, 1, 3, 2)
EPS = 1e-5
RIGHT, LEFT, GATHER, ADD, BACK, SENT, LOAD = 0, 4, 5, 17, 21, 22, 27


def nt(a, b):
    return lax.dot_general(a, b, (((1,), (1,)), ((), ())), preferred_element_type=F32)


def sigmoid(v):
    return 1.0 / (1.0 + jnp.exp(-v))


def wait_bytes(ref, sem):
    pltpu.make_async_copy(ref, ref, sem).wait()


def kernel(
    pair_hbm, gin_hbm, win_hbm, wgate_hbm, wout_hbm, gmid_hbm, len_hbm, allowed_hbm, out,
    pair, gin, win, wgate, wout, gmid, chain_len, allowed,
    gate, wt, stage, send_r, send_l, recv_r, recv_l, left, right, part, other, back, home, final, sems,
):
    row, col = lax.axis_index("row"), lax.axis_index("col")
    z, x = lax.div(row, NX), lax.rem(row, NX)
    y, core = lax.div(col, 2), lax.rem(col, 2)
    zp, zb = lax.div(z, 2), lax.rem(z, 2)
    xh, xl = lax.div(x, 2), lax.rem(x, 2)
    me = z * NY + y

    def chip(ty, tz):
        return (tz * NX + x, ty * 2 + core)

    def remote(src, dst, sent, arrived, there):
        return pltpu.make_async_remote_copy(
            src, dst, sems.at[sent], sems.at[arrived], device_id=there, device_id_type=MESH
        )

    beside = (row, col + 1 - 2 * core)
    along = [(d, (z * NX + lax.rem(x + d, NX), col)) for d in (2, 1, 3)]

    loads = [
        pltpu.make_async_copy(src, dst, sems.at[LOAD + n])
        for n, (src, dst) in enumerate(
            [(pair_hbm, pair), (gin_hbm, gin), (win_hbm, win), (wgate_hbm, wgate), (wout_hbm, wout),
             (gmid_hbm, gmid), (len_hbm, chain_len), (allowed_hbm, allowed)]
        )
    ]
    for load in loads:
        load.start()

    ring = [(dy, dz) for dy in range(NY) for dz in range(NZ) if dy or dz]
    ring.sort(key=lambda o: -min(o[0], NY - o[0]) - min(o[1], NZ - o[1]))
    barrier = pltpu.get_barrier_semaphore()
    for dy, dz in ring:
        there = chip(lax.rem(y + dy, NY), lax.rem(z + dz, NZ))
        pl.semaphore_signal(barrier, inc=1, device_id=there, device_id_type=MESH)
    for there in [beside] + [there for _, there in along]:
        pl.semaphore_signal(barrier, inc=1, device_id=there, device_id_type=MESH)

    lane = lax.broadcasted_iota(jnp.int32, (8, 128), 1)
    low = lane < 64
    lane32 = jnp.where(low, lane, lane - 64)
    even = lane32 < 32
    lane32 = jnp.where(even, lane32, lane32 - 32)

    def half_roll(v):
        return pltpu.roll(v, 64, 1)

    loads[0].wait()
    loads[1].wait()
    values = pair[...].reshape(512, 128).astype(F32)
    mean = jnp.mean(values, axis=1, keepdims=True)
    centered = values - mean
    var = jnp.mean(centered * centered, axis=1, keepdims=True)
    normed = (centered * lax.rsqrt(var + EPS) * gin[...]).astype(BF16)
    loads[2].wait()
    for b in range(4):
        wt[b * 128 : (b + 1) * 128, :] = win[:, b * 128 : (b + 1) * 128].astype(F32).T.astype(BF16)
    for load in loads[3:]:
        load.wait()

    column = col * 32 + lane32
    chain_row, chain_col, end = jnp.int32(0), jnp.zeros((8, 128), jnp.int32), jnp.int32(0)
    for c in range(3):
        end = end + chain_len[c]
        chain_row = chain_row + jnp.where(row >= end, 1, 0)
        chain_col = chain_col + jnp.where(column >= end * 16, 1, 0)
    mask = jnp.zeros((8, 128), F32)
    for b in range(4):
        pick = jnp.int32(0)
        for a in range(4):
            pick = jnp.where(chain_row == a, allowed[a, b], pick)
        mask = jnp.where(chain_col == b, pick.astype(F32), mask)
    mask = mask[0:1]

    wide_low = lax.broadcasted_iota(jnp.int32, (64, 128), 1) < 64

    def project(first, store):
        weights = wt[first * 128 : (first + 2) * 128, :]
        for t in range(0, 8, 2):
            four = [normed[i * 32 : (i + 1) * 32] for i in (t, 8 + t, t + 1, 9 + t)]
            proj = nt(weights, jnp.concatenate(four, axis=0))
            gated = sigmoid(proj[:128]) * proj[128:] * mask
            one, two = gated[:64], gated[64:]
            stage[pl.ds(t, 64, stride=8), :] = jnp.where(wide_low, one, half_roll(two))
            stage[pl.ds(t + 1, 64, stride=8), :] = jnp.where(wide_low, half_roll(one), two)
        store[...] = stage[...].reshape(64, 8, 128).astype(BF16)

    project(2, send_r)
    project(0, send_l)
    gate[...] = sigmoid(jnp.dot(normed, wgate[...], preferred_element_type=F32)).reshape(16, 32, 128)
    gain = jnp.broadcast_to(gmid[...], (128, 128)).T

    pl.semaphore_wait(barrier, NG + 3)
    for dy, dz in ring:
        ty, tz = lax.rem(y + dy, NY), lax.rem(z + dz, NZ)
        remote(send_r.at[tz * NY + ty], recv_r.at[zp, zb, y], SENT, RIGHT + zp, chip(ty, tz)).start()
    pltpu.make_async_copy(send_r.at[me], recv_r.at[zp, zb, y], sems.at[RIGHT + zp]).start()
    for dy, dz in ring:
        ty, tz = lax.rem(y + dy, NY), lax.rem(z + dz, NZ)
        remote(send_l.at[tz * NY + ty], recv_l.at[z, y], SENT + 1, LEFT, chip(ty, tz)).start()
    pltpu.make_async_copy(send_l.at[me], recv_l.at[z, y], sems.at[LEFT]).start()

    def merge(tiles):
        tiles = [tile.astype(F32) for tile in tiles]
        made = []
        for b in range(4):
            moved = [t if s == b else pltpu.roll(t, (s - b) % 4 * 32, 1) for s, t in enumerate(tiles)]
            made.append(jnp.where(low, jnp.where(even, moved[0], moved[1]), jnp.where(even, moved[2], moved[3])))
        return [jnp.concatenate(made[c * 2 : c * 2 + 2], axis=0).astype(BF16) for c in range(2)]

    def spread(p):
        wait_bytes(recv_r.at[p], sems.at[RIGHT + p])
        for b in range(2):
            for q in range(2):
                both = merge([recv_r[p, b, 4 * q + s] for s in range(4)])
                for c in range(2):
                    right[p, xh, b, xl, c, :, q * 128 : (q + 1) * 128] = both[c]
        own = right.at[p, xh, :, xl]
        for d, there in along:
            remote(own, own, SENT + 2, GATHER + 3 * p + d - 1, there).start()

    def contract(p):
        for d, _ in along:
            source = lax.rem(x + NX - d, NX)
            wait_bytes(right.at[p, lax.div(source, 2), :, lax.rem(source, 2)], sems.at[GATHER + 3 * p + d - 1])
        one, two = [
            nt(left[c].reshape(128, 256), right[p, :, :, :, c].reshape(128, 256)) for c in range(2)
        ]
        first = lax.broadcasted_iota(jnp.int32, (128, 128), 1) < 64
        part[p, 0] = jnp.where(first, one, half_roll(two))
        part[p, 1] = jnp.where(first, half_roll(one), two)
        remote(part.at[p, 1 - core], other.at[p], SENT + 3, ADD + p, beside).start()

    def finish(p):
        wait_bytes(other.at[p], sems.at[ADD + p])
        for zz in range(8):
            top, low_rows = slice(zz * 16, zz * 16 + 8), slice(zz * 16 + 8, zz * 16 + 16)
            one = part[p, core, top, :] + other[p, top, :]
            two = part[p, core, low_rows, :] + other[p, low_rows, :]
            back[p, 0, zz] = jnp.where(even, one, pltpu.roll(two, 32, 1)).astype(BF16)
            back[p, 1, zz] = jnp.where(even, pltpu.roll(one, 96, 1), two).astype(BF16)

        def give_back(b, tz):
            remote(back.at[p, b, tz], home.at[me], SENT + 4, BACK, chip(p * 2 + b, tz)).start()

        for dz in (4, 3, 5, 2, 6, 1, 7):
            for b in range(2):
                give_back(b, lax.rem(z + dz, NZ))
        for b in range(2):

            @pl.when(p * 2 + b != y)
            def _(b=b):
                give_back(b, z)

    c0, c1, c2, c3 = ORDER
    for p in ORDER:
        spread(p)
    wait_bytes(recv_l, sems.at[LEFT])
    for zz in range(8):
        for q in range(2):
            both = merge([recv_l[zz, 4 * q + s] for s in range(4)])
            for c in range(2):
                left[c, zz, :, q * 128 : (q + 1) * 128] = both[c]
    contract(c0)
    contract(c1)
    finish(c0)
    contract(c2)
    finish(c1)
    contract(c3)
    finish(c2)
    finish(c3)
    pltpu.make_async_copy(back.at[lax.div(y, 2), lax.rem(y, 2), z], home.at[me], sems.at[BACK]).start()
    wait_bytes(home, sems.at[BACK])

    final[...] = home[...].reshape(512, 128).astype(F32)
    for t in range(0, 8, 2):
        one, two = final[pl.ds(t, 64, stride=8), :], final[pl.ds(t + 1, 64, stride=8), :]
        mixed = jnp.concatenate(
            [jnp.where(wide_low, one, half_roll(two)), jnp.where(wide_low, half_roll(one), two)], axis=0
        )
        mean = jnp.mean(mixed, axis=0, keepdims=True)
        centered = mixed - mean
        var = jnp.mean(centered * centered, axis=0, keepdims=True)
        mixed_norm = (centered * lax.rsqrt(var + EPS) * gain).astype(BF16)
        rows = lax.dot_general(
            mixed_norm, wout[...], (((0,), (0,)), ((), ())), preferred_element_type=F32
        )
        for n, i in enumerate((t, 8 + t, t + 1, 9 + t)):
            out[i] = (gate[i] * rows[n * 32 : (n + 1) * 32]).astype(BF16)

    wait_bytes(send_r.at[pl.ds(0, NG - 1)], sems.at[SENT])
    wait_bytes(send_l.at[pl.ds(0, NG - 1)], sems.at[SENT + 1])
    for p in range(3):
        wait_bytes(right.at[p], sems.at[SENT + 2])
    wait_bytes(other, sems.at[SENT + 3])
    wait_bytes(send_l.at[pl.ds(0, NG - 1)], sems.at[SENT + 4])


def on_device(pair, gain_in, w_in, w_gate, w_out, gain_mid, chain_len, allowed):
    operands = (pair, gain_in.reshape(1, 128), w_in, w_gate, w_out, gain_mid.reshape(1, 128))
    scalars = (chain_len, allowed)
    return pl.pallas_call(
        kernel,
        out_shape=jax.ShapeDtypeStruct(pair.shape, pair.dtype),
        in_specs=[pl.BlockSpec(memory_space=pl.ANY)] * 8,
        out_specs=pl.BlockSpec(memory_space=pltpu.VMEM),
        scratch_shapes=[
            *[pltpu.VMEM(a.shape, a.dtype) for a in operands],
            *[pltpu.SMEM(a.shape, a.dtype) for a in scalars],
            pltpu.VMEM((16, 32, 128), F32),
            pltpu.VMEM((512, 128), BF16),
            pltpu.VMEM((512, 128), F32),
            pltpu.VMEM((NG, 8, 128), BF16),
            pltpu.VMEM((NG, 8, 128), BF16),
            pltpu.VMEM((4, 2, NY, 8, 128), BF16),
            pltpu.VMEM((NZ, NY, 8, 128), BF16),
            pltpu.VMEM((2, NZ, 16, 256), BF16),
            pltpu.VMEM((4, 2, 2, 2, 2, 16, 256), BF16),
            pltpu.VMEM((4, 2, 128, 128), F32),
            pltpu.VMEM((4, 128, 128), F32),
            pltpu.VMEM((4, 2, NZ, 8, 128), BF16),
            pltpu.VMEM((NG, 8, 128), BF16),
            pltpu.VMEM((512, 128), F32),
            pltpu.SemaphoreType.DMA((LOAD + 8,)),
        ],
        compiler_params=pltpu.CompilerParams(
            collective_id=0, has_side_effects=True, vmem_limit_bytes=32 * 2**20
        ),
    )(*[pltpu.with_memory_space_constraint(a, pltpu.HBM) for a in (*operands, *scalars)])


def solution(mesh):
    return jax.shard_map(
        on_device,
        mesh=mesh,
        in_specs=(P("row", "col", None), P(), P(), P(), P(), P(), P(), P()),
        out_specs=P("row", "col", None),
        check_vma=False,
    )
```

time: 42.5 us -> 38.6 us (0.908)
  Pallas kernels: 41.7 us -> 37.8 us
    pallas_call x1, Pallas kernels: 41.7 us -> 37.8 us  [on_device(): pl.pallas_call(kernel, out_shape=jax.ShapeDtypeStruct(pair.shape, pair.dt...]
where the time goes in v4:
time: 38.6 us; the launch traced here: 38.5 us
  Pallas kernels  37.8 us (98%)
  local copies, waits for them, and re-layouts  0.66 us (2%)
    pallas_call x1, Pallas kernels, on_device(): pl.pallas_call(kernel, out_shape=jax.ShapeDtypeStruct(pair.shape, pair.dt...  37.8 us

profile of v4, /device:TPU:1, one launch (start us, length us, event | category | flops | bytes accessed | tf_op | source)
XLA Modules:
  0.0 38.5 jit_solution(1921714977285615544)
XLA Ops:
  0.0 37.8 %shard_map.82 = bf16[16,32,128]{2,1,0:T(8,128)(2,1)S(1)} custom-call(bf16[16,32,128]{2,1,0:T(8,128)(2,1)} %pair_hbm.1, f32[1,128]{1,0:T(1,128)} %bitcast.2, bf16[128,512]{1,0:T(8,128)(2,1)} %win_hbm.1, bf16[128,128]{1,0:T(8,128)(2,1)} %wgate_hbm.1, bf16[128,128]{1,0:T(8,128)(2,1)} %wout_hbm.1, f32[1,128]{1,0:T(1,128)} %bitcast.3, s32[4]{0:T(128)} %len_hbm.1, ...), custom_call_target="tpu_custom_call" | custom-call | tf_op jit(solution)/shard_map/pallas_call | solution.py:234
  37.8 0.7 %copy.10 = bf16[16,32,128]{2,1,0:T(8,128)(2,1)} copy(bf16[16,32,128]{2,1,0:T(8,128)(2,1)S(1)} %shard_map.82) | data formatting | bytes 262144

commit v5 on v4

--- a/solution.py
+++ b/solution.py
@@ -147,21 +147,23 @@
                 both = merge([recv_r[p, b, 4 * q + s] for s in range(4)])
                 for c in range(2):
                     right[p, xh, b, xl, c, :, q * 128 : (q + 1) * 128] = both[c]
-        own = right.at[p, xh, :, xl]
-        for d, there in along:
-            remote(own, own, SENT + 2, GATHER + 3 * p + d - 1, there).start()
+            own = right.at[p, xh, b, xl]
+            for d, there in along:
+                remote(own, own, SENT + 2, GATHER + 3 * p + d - 1, there).start()
 
     def contract(p):
-        for d, _ in along:
-            source = lax.rem(x + NX - d, NX)
-            wait_bytes(right.at[p, lax.div(source, 2), :, lax.rem(source, 2)], sems.at[GATHER + 3 * p + d - 1])
-        one, two = [
-            nt(left[c].reshape(128, 256), right[p, :, :, :, c].reshape(128, 256)) for c in range(2)
-        ]
-        first = lax.broadcasted_iota(jnp.int32, (128, 128), 1) < 64
-        part[p, 0] = jnp.where(first, one, half_roll(two))
-        part[p, 1] = jnp.where(first, half_roll(one), two)
-        remote(part.at[p, 1 - core], other.at[p], SENT + 3, ADD + p, beside).start()
+        for half in (1 - core, core):
+            for e in range(2):
+                d = lax.rem(x - (2 * half + e) + NX, NX)
+
+                @pl.when(d > 0)
+                def _(half=half, e=e, d=d):
+                    wait_bytes(right.at[p, half, :, e], sems.at[GATHER + 3 * p + d - 1])
+
+            both = [nt(left[c].reshape(128, 256), right[p, half, :, :, c].reshape(64, 256)) for c in range(2)]
+            part[p, half] = jnp.concatenate(both, axis=1)
+            if half is not core:
+                remote(part.at[p, half], other.at[p], SENT + 3, ADD + p, beside).start()
 
     def finish(p):
         wait_bytes(other.at[p], sems.at[ADD + p])

time: 38.6 us -> 38.6 us (level)
  no operation moved by 1% of the time
where the time goes in v5:
time: 38.6 us; the launch traced here: 38.5 us
  Pallas kernels  37.8 us (98%)
  local copies, waits for them, and re-layouts  0.66 us (2%)
    pallas_call x1, Pallas kernels, on_device(): pl.pallas_call(kernel, out_shape=jax.ShapeDtypeStruct(pair.shape, pair.dt...  37.8 us

profile of v5, /device:TPU:1, one launch (start us, length us, event | category | flops | bytes accessed | tf_op | source)
XLA Modules:
  0.0 38.5 jit_solution(7798500738011556497)
XLA Ops:
  0.0 37.8 %shard_map.82 = bf16[16,32,128]{2,1,0:T(8,128)(2,1)S(1)} custom-call(bf16[16,32,128]{2,1,0:T(8,128)(2,1)} %pair_hbm.1, f32[1,128]{1,0:T(1,128)} %bitcast.2, bf16[128,512]{1,0:T(8,128)(2,1)} %win_hbm.1, bf16[128,128]{1,0:T(8,128)(2,1)} %wgate_hbm.1, bf16[128,128]{1,0:T(8,128)(2,1)} %wout_hbm.1, f32[1,128]{1,0:T(1,128)} %bitcast.3, s32[4]{0:T(128)} %len_hbm.1, ...), custom_call_target="tpu_custom_call" | custom-call | tf_op jit(solution)/shard_map/pallas_call | solution.py:236
  37.8 0.7 %copy.10 = bf16[16,32,128]{2,1,0:T(8,128)(2,1)} copy(bf16[16,32,128]{2,1,0:T(8,128)(2,1)S(1)} %shard_map.82) | data formatting | bytes 262144
